TPU v7x, 32 devices: a whole 2x2x4 slice. The times are simulated.
32 devices in a mesh: dp: 8 (over y, x, core), tensor: 4 (over z).
Axes of the slice: x: 2, y: 2, z: 4, core: 2. Of those that a mesh axis runs over, the one named last changes fastest.
Arguments:
- tokens: bfloat16 [16384, 768], P(('dp', 'tensor')), may hold values from -6 to 6
- cotangent: bfloat16 [16384, 768], P(('dp', 'tensor')), may hold values from -6 to 6, as said below
- segment: int32 [32, 512], P(('dp', 'tensor')), may hold values from 0 to 11, never falling along the last dimension, each value on 1 to 202 neighbouring positions
- projection: float32 [64, 32], replicated, may hold values from -5 to 5
- first_gain: float32 [768], replicated, may hold values from 0.5 to 1.5
- first_bias: float32 [768], replicated, may hold values from -4 to 4
- w_query: bfloat16 [768, 768], replicated, may hold values from -0.109375 to 0.109375
- w_key: bfloat16 [768, 768], replicated, may hold values from -0.109375 to 0.109375
- w_value: bfloat16 [768, 768], replicated, may hold values from -0.21875 to 0.21875
- w_out: bfloat16 [768, 768], replicated, may hold values from -1.25 to 1.25
- b_query: float32 [768], replicated, may hold values from -4 to 4
- b_key: float32 [768], replicated, may hold values from -4 to 4
- b_value: float32 [768], replicated, may hold values from -4 to 4
- b_out: float32 [768], replicated, may hold values from -4 to 4
- second_gain: float32 [768], replicated, may hold values from 0.5 to 1.5
- second_bias: float32 [768], replicated, may hold values from -4 to 4
- w_up: bfloat16 [768, 3072], P(None, 'tensor'), may hold values from -0.21875 to 0.21875
- b_up: float32 [3072], P('tensor'), may hold values from -4 to 4
- w_down: bfloat16 [3072, 768], P('tensor'), may hold values from -0.109375 to 0.109375
- b_down: float32 [768], replicated, may hold values from -4 to 4
Outputs:
- output: bfloat16 [16384, 768], P(('dp', 'tensor'))
- grad_tokens: bfloat16 [16384, 768], P(('dp', 'tensor'))
- grad_first_gain: float32 [768], replicated
- grad_first_bias: float32 [768], replicated
- grad_w_query: float32 [768, 768], replicated
- grad_w_key: float32 [768, 768], replicated
- grad_w_value: float32 [768, 768], replicated
- grad_w_out: float32 [768, 768], replicated
- grad_b_query: float32 [768], replicated
- grad_b_key: float32 [768], replicated
- grad_b_value: float32 [768], replicated
- grad_b_out: float32 [768], replicated
- grad_second_gain: float32 [768], replicated
- grad_second_bias: float32 [768], replicated
- grad_w_up: float32 [768, 3072], P(None, 'tensor')
- grad_b_up: float32 [3072], P('tensor')
- grad_w_down: float32 [3072, 768], P('tensor')
- grad_b_down: float32 [768], replicated
Inputs may be any that keep to these rules, and one draw needn't show every extreme that they name: `segment`: within each row of 512 tokens, molecule numbers never fall; each molecule has 1 to 202 tokens and one has exactly 202. `cotangent`: gradient rows of order one.
All inputs are finite; a program needn't handle non-finite values.
Results may differ from a plain program's by a relative error of at most 0.01.
Values may be sent and summed in bfloat16 or wider, within the bound.
No kernel may reach another device: no remote copies, remote signals or barrier semaphores. Data moves between devices by JAX's collectives and lax.ppermute only.
A program may use at most 192 MiB of HBM per device.

v0:
```python
from functools import partial
import math

import jax
import jax.numpy as jnp
from jax import lax
from jax.sharding import PartitionSpec as P

HEADS = 12


highest_precision = lax.Precision.HIGHEST


def layer_norm(inputs, gain, shift):
    average = jnp.mean(inputs, -1, keepdims=True)
    centred = inputs - average
    spread = jnp.mean(centred * centred, -1, keepdims=True)
    return centred * lax.rsqrt(spread + 1e-05) * gain + shift


def positions(labels):
    places = jnp.arange(labels.shape[0], dtype=jnp.int32)
    matches = labels[:, None] == labels[None, :]
    before = places[None, :] < places[:, None]
    return jnp.sum((matches & before).astype(jnp.int32), axis=1)


def rotate(inputs, places):
    split_at = inputs.shape[-1] // 2
    ladder = jnp.arange(split_at).astype(jnp.float32)
    speeds = jnp.exp(ladder * (-2.0 * math.log(10000.0) / inputs.shape[-1]))
    angles = places.astype(jnp.float32)[:, None] * speeds[None, :]
    cosine = jnp.cos(angles)[:, None, :]
    sine_part = jnp.sin(angles)[:, None, :]
    lower_half = inputs[..., :split_at]
    upper_half = inputs[..., split_at:]
    return jnp.concatenate(
        [
            lower_half * cosine - upper_half * sine_part,
            upper_half * cosine + lower_half * sine_part,
        ],
        -1,
    )


def features(inputs, projection):
    scaled = inputs * inputs.shape[-1] ** (-0.25)
    projected = jnp.einsum("rhd,df->rhf", scaled, projection, precision=highest_precision)
    return jnp.exp(
        projected - 0.5 * jnp.sum(scaled * scaled, -1, keepdims=True)
    ) * projection.shape[-1] ** (-0.5)


def attend(queries, key_rows, value_rows, labels, projection):
    row_count = queries.shape[0]
    places = positions(labels)
    query_feature_map = features(rotate(queries.reshape(row_count, HEADS, -1), places), projection)
    key_feature_map = features(rotate(key_rows.reshape(row_count, HEADS, -1), places), projection)
    value_heads = value_rows.reshape(row_count, HEADS, -1)
    attention_scores = jnp.einsum(
        "otg,atg->toa", query_feature_map, key_feature_map, precision=highest_precision
    )
    matches = (labels[:, None] == labels[None, :]).astype(attention_scores.dtype)
    weights = attention_scores * matches[None]
    totals = jnp.sum(weights, -1)
    mixture = jnp.einsum("hqk,khd->qhd", weights, value_heads, precision=highest_precision)
    return (mixture / jnp.transpose(totals)[:, :, None]).reshape(row_count, -1)


def matmul(left, right):
    return jnp.dot(left, right, preferred_element_type=jnp.float32)


def left_product(left, right):
    return lax.dot_general(
        left, right, (((0,), (0,)), ((), ())), preferred_element_type=jnp.float32
    )


def right_product(left, right):
    return lax.dot_general(
        left, right, (((1,), (1,)), ((), ())), preferred_element_type=jnp.float32
    )


def column_sum(values):
    return jnp.sum(values.astype(jnp.float32), 0)


def body(
    tokens,
    cotangent,
    segment,
    projection,
    first_gain,
    first_bias,
    w_query,
    w_key,
    w_value,
    w_out,
    b_query,
    b_key,
    b_value,
    b_out,
    second_gain,
    second_bias,
    w_up,
    b_up,
    w_down,
    b_down,
):
    row_count = tokens.shape[0]
    labels = segment[0]
    widened = tokens.astype(jnp.float32)
    normed, first_back = jax.vjp(layer_norm, widened, first_gain, first_bias)
    normed_low = normed.astype(jnp.bfloat16)
    queries = matmul(normed_low, w_query) + b_query
    key_rows = matmul(normed_low, w_key) + b_key
    value_rows = matmul(normed_low, w_value) + b_value

    def attend_here(query_in, key_in, value_in):
        return attend(query_in, key_in, value_in, labels, projection)

    context, kernel_core_pullback = jax.vjp(attend_here, queries, key_rows, value_rows)
    context_low = context.astype(jnp.bfloat16)
    middle = widened + matmul(context_low, w_out) + b_out
    second, second_back = jax.vjp(layer_norm, middle, second_gain, second_bias)
    second_low = second.astype(jnp.bfloat16)
    upstream = cotangent.astype(jnp.float32)
    down_bias_grad = jnp.sum(upstream, 0)
    gathered = lax.all_gather(second_low, "tensor", axis=0, tiled=True)
    inner_rows = matmul(gathered, w_up) + b_up
    hidden, gelu_back = jax.vjp(partial(jax.nn.gelu, approximate=False), inner_rows)
    hidden_low = hidden.astype(jnp.bfloat16)
    branch = lax.psum_scatter(
        matmul(
            lax.slice_in_dim(hidden_low, 0, row_count * lax.axis_size("tensor"), axis=0), w_down
        ).astype(jnp.bfloat16),
        "tensor",
        scatter_dimension=0,
        tiled=True,
    ).astype(jnp.float32)
    output = (middle + branch + b_down).astype(jnp.bfloat16)
    cot_gathered = lax.all_gather(cotangent, "tensor", axis=0, tiled=True)
    down_grad = left_product(hidden_low, cot_gathered)
    hidden_grad = right_product(cot_gathered, w_down)
    inner_grad = gelu_back(hidden_grad)[0].astype(jnp.bfloat16)
    up_bias_grad = column_sum(inner_grad)
    up_grad = left_product(gathered, inner_grad)
    second_grad = lax.psum_scatter(
        right_product(inner_grad, w_up).astype(jnp.bfloat16),
        "tensor",
        scatter_dimension=0,
        tiled=True,
    ).astype(jnp.float32)
    up_grad, up_bias_grad, down_grad = lax.psum((up_grad, up_bias_grad, down_grad), "dp")
    middle_back, gain_two_grad, bias_two_grad = second_back(second_grad)
    middle_grad = upstream + middle_back
    out_grad_low = middle_grad.astype(jnp.bfloat16)
    wout_grad = left_product(context_low, out_grad_low)
    bout_grad = column_sum(out_grad_low)
    context_grad = right_product(out_grad_low, w_out)
    query_grad, key_grad, value_grad = kernel_core_pullback(context_grad)
    query_low = query_grad.astype(jnp.bfloat16)
    key_low = key_grad.astype(jnp.bfloat16)
    value_low = value_grad.astype(jnp.bfloat16)
    query_weight_grad = left_product(normed_low, query_low)
    wkey_grad = left_product(normed_low, key_low)
    value_weight_grad = left_product(normed_low, value_low)
    bquery_grad = column_sum(query_low)
    bkey_grad = column_sum(key_low)
    bvalue_grad = column_sum(value_low)
    normed_grad = (
        right_product(query_low, w_query)
        + right_product(key_low, w_key)
        + right_product(value_low, w_value)
    )
    token_back, gain_one_grad, bias_one_grad = first_back(normed_grad)
    grad_tokens = (middle_grad + token_back).astype(jnp.bfloat16)
    (
        gain_one_grad,
        bias_one_grad,
        query_weight_grad,
        wkey_grad,
        value_weight_grad,
        wout_grad,
        bquery_grad,
        bkey_grad,
        bvalue_grad,
        bout_grad,
        gain_two_grad,
        bias_two_grad,
        down_bias_grad,
    ) = lax.psum(
        (
            gain_one_grad,
            bias_one_grad,
            query_weight_grad,
            wkey_grad,
            value_weight_grad,
            wout_grad,
            bquery_grad,
            bkey_grad,
            bvalue_grad,
            bout_grad,
            gain_two_grad,
            bias_two_grad,
            down_bias_grad,
        ),
        ("dp", "tensor"),
    )
    return (
        output,
        grad_tokens,
        gain_one_grad,
        bias_one_grad,
        query_weight_grad,
        wkey_grad,
        value_weight_grad,
        wout_grad,
        bquery_grad,
        bkey_grad,
        bvalue_grad,
        bout_grad,
        gain_two_grad,
        bias_two_grad,
        up_grad,
        up_bias_grad,
        down_grad,
        down_bias_grad,
    )


def solution(mesh):
    return jax.shard_map(
        body,
        mesh=mesh,
        in_specs=(
            P(("dp", "tensor"), None),
            P(("dp", "tensor"), None),
            P(("dp", "tensor"), None),
            P(),
            P(),
            P(),
            P(),
            P(),
            P(),
            P(),
            P(),
            P(),
            P(),
            P(),
            P(),
            P(),
            P(None, "tensor"),
            P("tensor"),
            P("tensor", None),
            P(),
        ),
        out_specs=(
            P(("dp", "tensor"), None),
            P(("dp", "tensor"), None),
            P(),
            P(),
            P(),
            P(),
            P(),
            P(),
            P(),
            P(),
            P(),
            P(),
            P(),
            P(),
            P(None, "tensor"),
            P("tensor"),
            P("tensor", None),
            P(),
        ),
        check_vma=False,
    )
```

profile of v0, /device:TPU:0, one launch (start us, length us, event | category | flops | bytes accessed | tf_op | source)
XLA Modules:
  0.0 651.4 jit_solution(13527128081990880448)
XLA Ops:
  11.9 3.0 copy.50
  14.9 3.3 convolution_add_fusion
  34.1 12.6 %multiply_reduce_fusion = (f32[12,512]{1,0:T(8,128)S(1)}, f32[12,512,512]{1,2,0:T(8,128)S(1)}) fusion(f32[512,512]{0,1:T(8,128)S(1)} %compare_convert_fusion, f32[512,12,32]{0,2,1:T(8,128)} %fusion.59, f32[512,12,32]{0,2,1:T(8,128)} %fusion.53), kind=kOutput, calls=%fused_computation.5 | convolution fusion | flops 1214638080 | bytes 15228928 | tf_op jit(solution)/shard_map/jvp(otg,atg->toa)/dot_general | solution.py:61
  46.7 9.7 %fusion.37 = (bf16[512,12,64]{0,2,1:T(8,128)(2,1)S(1)}, f32[12,64,512]{2,1,0:T(8,128)}) fusion(f32[512,12]{0,1:T(8,128)S(1)} %bitcast.95, f32[512,12,64]{0,2,1:T(8,128)S(1)} %bitcast.84, f32[12,512,512]{1,2,0:T(8,128)S(1)} %get-tuple-element.69, f32[512,512]{0,1:T(8,128)S(1)} %compare_convert_fusion), kind=kOutput, calls=%fused_computation.67 | convolution fusion | flops 2419851264 | bytes 17588224 | tf_op jit(solution)/shard_map/jvp(hqk,khd->qhd)/dot_general | solution.py:67
  60.5 65.5 %all-gather.3.cloned.1.call-done = bf16[2048,768]{1,0:T(8,128)(2,1)} async-done(((bf16[512,768]{1,0:T(8,128)(2,1)}), bf16[2048,768]{1,0:T(8,128)(2,1)}) %all-gather.3.cloned.1.call-update) | async-done | bytes 3145744 | tf_op jit(solution)/shard_map/all_gather | solution.py:132
  126.1 7.4 %fusion.109 = f32[2048,768]{1,0:T(8,128)} fusion(bf16[2048,768]{1,0:T(8,128)(2,1)} %all-gather.3.cloned.1.call-done, bf16[768,768]{1,0:T(8,128)(2,1)} %param.36), kind=kOutput, calls=%fused_computation.167 | convolution fusion | flops 2415919104 | bytes 10616832 | tf_op jit(solution)/shard_map/dot_general | solution.py:72
  133.5 56.3 %all-gather.5.cloned.1.call-done = bf16[2048,768]{1,0:T(8,128)(2,1)} async-done(((bf16[512,768]{1,0:T(8,128)(2,1)}), bf16[2048,768]{1,0:T(8,128)(2,1)}) %all-gather.5.cloned.1.call-update) | async-done | bytes 3145744 | tf_op jit(solution)/shard_map/all_gather | solution.py:145
  189.8 19.6 %convert_reduce_fusion = (f32[768]{0:T(1024)S(1)}, bf16[2048,768]{1,0:T(8,128)(2,1)S(1)}, f32[2048,768]{1,0:T(8,128)}) fusion(f32[2048,768]{1,0:T(8,128)} %fusion.109, f32[768]{0:T(1024)S(1)} %copy-done.41, bf16[2048,768]{1,0:T(8,128)(2,1)} %all-gather.5.cloned.1.call-done, bf16[768,768]{1,0:T(8,128)(2,1)S(1)} %copy-done), kind=kOutput, calls=%fused_computation.10 | convolution fusion | flops 2533883136 | bytes 20060160 | tf_op jit(solution)/shard_map/dot_general | solution.py:82
  211.2 4.0 convolution_convert_fusion
  215.3 5.5 multiply_convert_fusion
  222.4 3.9 convolution_convert_fusion.1
  226.5 7.1 %fusion.114 = f32[768,768]{1,0:T(8,128)} fusion(bf16[2048,768]{1,0:T(8,128)(2,1)} %all-gather.3.cloned.1.call-done, bf16[2048,768]{1,0:T(8,128)(2,1)} %copy-done.54), kind=kOutput, calls=%fused_computation.172 | convolution fusion | flops 2415919104 | bytes 8650752 | tf_op jit(solution)/shard_map/dot_general | solution.py:76
  233.6 4.2 fusion.115
  238.3 36.0 %reduce-scatter.5.cloned.1.call-done = bf16[512,768]{1,0:T(8,128)(2,1)} async-done(((bf16[2048,768]{1,0:T(8,128)(2,1)}), bf16[512,768]{1,0:T(8,128)(2,1)}) %reduce-scatter.5.cloned.1.call-update) | async-done | bytes 786448 | tf_op jit(solution)/shard_map/reduce_scatter | solution.py:151
  276.6 60.1 %reduce-scatter.3.cloned.1.call-done = bf16[512,768]{1,0:T(8,128)(2,1)} async-done(((bf16[2048,768]{1,0:T(8,128)(2,1)}), bf16[512,768]{1,0:T(8,128)(2,1)}) %reduce-scatter.3.cloned.1.call-update) | async-done | bytes 786448 | tf_op jit(solution)/shard_map/reduce_scatter | solution.py:136
  336.7 3.5 fusion.105
  343.5 10.5 %fusion.35 = f32[12,512,512]{1,2,0:T(8,128)S(1)} fusion(f32[512,12,64]{0,2,1:T(8,128)S(1)} %bitcast.85, f32[512,12,64]{0,2,1:T(8,128)S(1)} %bitcast.86, f32[512,12]{0,1:T(8,128)S(1)} %bitcast.96), kind=kOutput, calls=%fused_computation.63 | convolution fusion | flops 2416312320 | bytes 15753216 | tf_op jit(solution)/shard_map/transpose(jvp(hqk,khd->qhd))/dot_general | solution.py:67
  355.4 8.6 %fusion.108 = (f32[512,12]{0,1:T(8,128)S(1)}, f32[512,12,32]{0,2,1:T(8,128)S(1)}) fusion(f32[512,12,32]{0,2,1:T(8,128)S(1)} %copy-done.9, f32[512,12,32]{0,2,1:T(8,128)S(1)} %copy-done.10, f32[12,512,512]{1,2,0:T(8,128)S(1)} %fusion.35, f32[12,512]{1,0:T(8,128)S(1)} %negate_bitcast_fusion, f32[512,512]{0,1:T(8,128)S(1)} %compare_convert_fusion), kind=kOutput, calls=%fused_computation.166 | convolution fusion | flops 1215031296 | bytes 16039936 | tf_op jit(solution)/shard_map/transpose(jvp(otg,atg->toa))/dot_general | solution.py:61
  364.1 12.9 %fusion.107 = (f32[512,12]{0,1:T(8,128)S(1)}, f32[512,12,32]{0,2,1:T(8,128)S(1)}) fusion(f32[512,12,32]{0,2,1:T(8,128)S(1)} %copy-done.10, f32[512,12,32]{0,2,1:T(8,128)S(1)} %copy-done.9, f32[12,512,512]{1,2,0:T(8,128)S(1)} %fusion.35, f32[12,512]{1,0:T(8,128)S(1)} %negate_bitcast_fusion, f32[512,512]{0,1:T(8,128)S(1)} %compare_convert_fusion), kind=kOutput, calls=%fused_computation.165 | convolution fusion | flops 1215031296 | bytes 16039936 | tf_op jit(solution)/shard_map/transpose(jvp(otg,atg->toa))/dot_general | solution.py:61
  390.6 12.1 %convert_reduce_fusion.5 = (f32[12,64]{1,0:T(8,128)S(1)}, bf16[12,64,512]{2,1,0:T(8,128)(2,1)S(1)}) fusion(f32[12,512,512]{1,2,0:T(8,128)S(1)} %bitcast.83, f32[512,512]{0,1:T(8,128)S(1)} %compare_convert_fusion, f32[512,12,64]{0,2,1:T(8,128)S(1)} %bitcast.88, f32[512,12]{0,1:T(8,128)S(1)} %bitcast.97), kind=kOutput, calls=%fused_computation.74 | convolution fusion | flops 2420636928 | bytes 16018432 | tf_op jit(solution)/shard_map/transpose(jvp(hqk,khd->qhd))/dot_general | solution.py:67
  405.2 14.8 %psum.125 = f32[768]{0:T(1024)} all-reduce(f32[768]{0:T(1024)S(1)} %get-tuple-element.40), channel_id=1, replica_groups=mesh['dp'=8,'tensor'=4] {'dp'}, use_global_device_ids=true, to_apply=%region_39.0 | all-reduce | flops 768 | bytes 6144 | tf_op jit(solution)/shard_map/psum | solution.py:157
  428.3 42.2 %all-reduce.4 = (f32[768]{0:T(1024)}, f32[768]{0:T(1024)}, f32[768]{0:T(1024)}, f32[768]{0:T(1024)}, f32[768]{0:T(1024)}, /*index=5*/f32[768]{0:T(1024)}, f32[768]{0:T(1024)}, f32[768]{0:T(1024)}, f32[768]{0:T(1024)}) all-reduce(f32[768]{0:T(1024)S(1)} %get-tuple-element.18, ...), channel_id=1, replica_groups=mesh['dp'=8,'tensor'=4] {'dp','tensor'}, use_global_device_ids=true, to_apply=%region_18.0 | all-reduce | flops 6912 | bytes 55296 | tf_op jit(solution)/shard_map/psum | solution.py:195
  470.5 159.0 %all-reduce.10.cloned.1.call-done = (f32[768,768]{1,0:T(8,128)}, f32[768,768]{1,0:T(8,128)}, f32[768,768]{1,0:T(8,128)}, f32[768,768]{1,0:T(8,128)}) async-done(((f32[768,768]{1,0:T(8,128)}, f32[768,768]{1,0:T(8,128)}, f32[768,768]{1,0:T(8,128)}, f32[768,768]{1,0:T(8,128)}), (f32[768,768]{1,0:T(8,128)}, f32[768,768]{1,0:T(8,128)}, f32[768,768]{1,0:T(8,128)}, ...) | async-done | bytes 9437200 | tf_op jit(solution)/shard_map/psum | solution.py:195
  629.5 3.4 copy.70
  (188 shorter events, 71.0 us)
Async XLA Ops:
  7.2 182.7 %copy-start = (bf16[768,768]{1,0:T(8,128)(2,1)S(1)}, bf16[768,768]{1,0:T(8,128)(2,1)}, u32[]{:S(2)}) copy-start(bf16[768,768]{1,0:T(8,128)(2,1)} %param.38) | copy-start | bytes 3538948
  7.2 118.8 %all-gather.3.cloned.1.call-start = ((), (), s32[]{:S(2)}) async-start(), calls=%async_computation.2 | async-start | bytes 3932160 | tf_op jit(solution)/shard_map/all_gather | solution.py:132
  34.1 12.6 %copy-start.7 = (f32[512,768]{0,1:T(8,128)S(1)}, f32[512,768]{0,1:T(8,128)}, u32[]{:S(2)}) copy-start(f32[512,768]{0,1:T(8,128)} %copy.49) | copy-start | bytes 4718596
  46.7 9.7 %copy-start.2 = (f32[12,512,512]{1,2,0:T(8,128)}, f32[12,512,512]{1,2,0:T(8,128)S(1)}, u32[]{:S(2)}) copy-start(f32[12,512,512]{1,2,0:T(8,128)S(1)} %get-tuple-element.69) | copy-start | bytes 37748740
  46.7 9.7 %copy-start.45 = (bf16[768,768]{1,0:T(8,128)(2,1)S(1)}, bf16[768,768]{1,0:T(8,128)(2,1)}, u32[]{:S(2)}) copy-start(bf16[768,768]{1,0:T(8,128)(2,1)} %param.29) | copy-start | bytes 3538948
  46.7 9.7 %copy-start.52 = (f32[768]{0:T(1024)S(1)}, f32[768]{0:T(1024)}, u32[]{:S(2)}) copy-start(f32[768]{0:T(1024)} %param.33) | copy-start | bytes 9220
  59.7 130.1 %all-gather.5.cloned.1.call-start = ((), (), s32[]{:S(2)}) async-start(), calls=%async_computation.4 | async-start | bytes 3932160 | tf_op jit(solution)/shard_map/all_gather | solution.py:145
  60.5 129.4 %copy-start.41 = (f32[768]{0:T(1024)S(1)}, f32[768]{0:T(1024)}, u32[]{:S(2)}) copy-start(f32[768]{0:T(1024)} %param.37) | copy-start | bytes 9220
  60.5 213.8 %reduce-scatter.5.cloned.1.call-start = ((), (), s32[]{:S(2)}) async-start(), calls=%async_computation.5 | async-start | bytes 3932160 | tf_op jit(solution)/shard_map/reduce_scatter | solution.py:151
  189.8 21.3 %copy-start.44 = (bf16[768,768]{1,0:T(8,128)(2,1)S(1)}, bf16[768,768]{1,0:T(8,128)(2,1)}, u32[]{:S(2)}) copy-start(bf16[768,768]{1,0:T(8,128)(2,1)} %param.36) | copy-start | bytes 3538948
  215.2 121.5 %reduce-scatter.3.cloned.1.call-start = ((), (), s32[]{:S(2)}) async-start(), calls=%async_computation.3 | async-start | bytes 3932160 | tf_op jit(solution)/shard_map/reduce_scatter | solution.py:136
  226.4 244.1 %all-reduce.12.cloned.1.call-start = ((), (), s32[]{:S(2)}) async-start(), calls=%async_computation.7 | async-start | bytes 9437184 | tf_op jit(solution)/shard_map/psum | solution.py:157
  226.5 7.2 %copy-start.25 = (bf16[2048,768]{1,0:T(8,128)(2,1)S(1)}, bf16[2048,768]{1,0:T(8,128)(2,1)}, u32[]{:S(2)}) copy-start(bf16[2048,768]{1,0:T(8,128)(2,1)} %copy-done.24) | copy-start | bytes 9437188
  226.5 7.1 %copy-start.43 = (bf16[2048,768]{1,0:T(8,128)(2,1)S(1)}, bf16[2048,768]{1,0:T(8,128)(2,1)}, u32[]{:S(2)}) copy-start(bf16[2048,768]{1,0:T(8,128)(2,1)} %all-gather.5.cloned.1.call-done) | copy-start | bytes 9437188
  237.8 98.9 %copy-start.42 = (f32[768]{0:T(1024)S(1)}, f32[768]{0:T(1024)}, u32[]{:S(2)}) copy-start(f32[768]{0:T(1024)} %param.39) | copy-start | bytes 9220
  237.8 391.7 %all-reduce.10.cloned.1.call-start = ((), (), s32[]{:S(2)}) async-start(), calls=%async_computation.6 | async-start | bytes 18874368 | tf_op jit(solution)/shard_map/psum | solution.py:195
  276.6 63.6 %copy-start.19 = (bf16[512,768]{1,0:T(8,128)(2,1)S(1)}, bf16[512,768]{1,0:T(8,128)(2,1)}, u32[]{:S(2)}) copy-start(bf16[512,768]{1,0:T(8,128)(2,1)} %param.21) | copy-start | bytes 2359300
  343.5 10.5 %copy-start.21 = (f32[12,64,512]{2,1,0:T(8,128)S(1)}, f32[12,64,512]{2,1,0:T(8,128)}, u32[]{:S(2)}) copy-start(f32[12,64,512]{2,1,0:T(8,128)} %get-tuple-element.71) | copy-start | bytes 4718596
  364.1 13.0 %copy-start.16 = (f32[512,12,32]{0,2,1:T(8,128)S(1)}, f32[512,12,32]{0,2,1:T(8,128)}, u32[]{:S(2)}) copy-start(f32[512,12,32]{0,2,1:T(8,128)} %copy-done.15) | copy-start | bytes 2359300
  364.1 13.0 %copy-start.18 = (f32[512,12,32]{0,2,1:T(8,128)S(1)}, f32[512,12,32]{0,2,1:T(8,128)}, u32[]{:S(2)}) copy-start(f32[512,12,32]{0,2,1:T(8,128)} %copy-done.17) | copy-start | bytes 2359300
  380.5 10.1 %slice-start = ((s8[12582912]{0:T(1024)(128)(4,1)}), s8[4194304]{0:T(1024)(128)(4,1)S(1)}, s32[]{:S(2)}) async-start(s8[12582912]{0:T(1024)(128)(4,1)} %bitcast.82), calls=%async_computation.8 | async-start | bytes 8388608
  381.2 9.4 %slice-start.1 = ((s8[12582912]{0:T(1024)(128)(4,1)}), s8[4194304]{0:T(1024)(128)(4,1)S(1)}, s32[]{:S(2)}) async-start(s8[12582912]{0:T(1024)(128)(4,1)} %bitcast.82), calls=%async_computation.9 | async-start | bytes 8388608
  385.1 5.4 slice-start.2
  405.2 15.0 %copy-start.34 = (bf16[512,12,64]{0,2,1:T(8,128)(2,1)S(1)}, bf16[512,12,64]{0,2,1:T(8,128)(2,1)}, u32[]{:S(2)}) copy-start(bf16[512,12,64]{0,2,1:T(8,128)(2,1)} %copy-done.33) | copy-start | bytes 2359300
  (40 other events, 83.6 us)
Sparse Core Ops, SparseCore 0:
  59.9 66.1 all-gather.2
  127.7 62.1 all-gather.4
  215.4 58.8 reduce-scatter.4
  276.4 60.2 reduce-scatter.2
  340.5 87.1 all-reduce.11
  436.6 192.8 all-reduce.9
where the time goes:
time: 661 us; the launch traced here: 651 us
  waiting for transfers between devices  378 us (57%)
  matrix products  144 us (22%)
  blocking collectives  57 us (9%)
  local copies, waits for them, and re-layouts  34.7 us (5%)
  other arithmetic  22.8 us (3%)
  between operations  15 us (2%)
    psum x1, waiting for transfers between devices, body(): lax.psum((gain_one_grad, bias_one_grad, query_weight_grad, wkey_grad, val...  159 us
    all_gather x1, waiting for transfers between devices, body(): gathered = lax.all_gather(second_low, 'tensor', axis=0, tiled=True)  65.5 us
    reduce_scatter x1, waiting for transfers between devices, body(): lax.psum_scatter(matmul(lax.slice_in_dim(hidden_low, 0, row_count * lax.a...  60.1 us
    all_gather x1, waiting for transfers between devices, body(): cot_gathered = lax.all_gather(cotangent, 'tensor', axis=0, tiled=True)  56.3 us
    psum x1, blocking collectives, body(): lax.psum((gain_one_grad, bias_one_grad, query_weight_grad, wkey_grad, val...  42.2 us
    reduce_scatter x1, waiting for transfers between devices, body(): lax.psum_scatter(right_product(inner_grad, w_up).astype(jnp.bfloat16), 't...  36 us
    dot_general x3, matrix products, attend(): jnp.einsum('otg,atg->toa', query_feature_map, key_feature_map, precision=...  34.1 us
    dot_general x3, matrix products, attend(): jnp.einsum('hqk,khd->qhd', weights, value_heads, precision=highest_precis...  32.3 us
  transfers between devices with their start and end apart: 6, of which 5 were waited for; matrix products, arithmetic and copies ran while one was open for 16% of the time, Pallas kernels for 0%

commit v1 on v0

v1 whole, which is shorter than its diff:
```python
from functools import partial
import math

import jax
import jax.numpy as jnp
import ml_dtypes
import numpy as np
from jax import lax
from jax.experimental import pallas as pl
from jax.experimental.pallas import tpu as pltpu
from jax.sharding import PartitionSpec as P

HEADS = 12
HD = 64
FEAT = 32
EPS = 1e-05
F32 = jnp.float32
BF16 = jnp.bfloat16
ANY = pl.BlockSpec(memory_space=pl.ANY)
SMEM = pl.BlockSpec(memory_space=pltpu.SMEM)
SCALE = HD ** -0.25


def nn(a, b):
    return lax.dot_general(a, b, (((1,), (0,)), ((), ())), preferred_element_type=F32)


def nt(a, b):
    return lax.dot_general(a, b, (((1,), (1,)), ((), ())), preferred_element_type=F32)


def split(v):
    high = v.astype(BF16)
    return high, (v - high.astype(F32)).astype(BF16)


def rotary_table(length):
    half = HD // 2
    rate = np.exp(np.arange(half) * (-2.0 * math.log(10000.0) / HD))
    angle = np.arange(length)[:, None] * rate[None, :]
    lane = np.arange(128)
    cos = np.tile(np.cos(angle), (1, 4)) * SCALE
    sin = np.tile(np.sin(angle), (1, 4)) * SCALE
    first = (lane % HD < half)[None, :]
    table = np.concatenate([cos, -sin * first, sin * ~first], 1).astype(np.float32)
    parts = []
    for _ in range(3):
        part = table.astype(ml_dtypes.bfloat16)
        parts.append(part)
        table = table - part.astype(np.float32)
    return np.stack(parts)


def lane_mask(head_in_group):
    lane = lax.broadcasted_iota(jnp.int32, (1, 128), 1)
    return jnp.where(lane // FEAT == head_in_group, 1.0, 0.0).astype(BF16)


def norm_parts(v):
    centred = v - jnp.mean(v, -1, keepdims=True)
    scale = lax.rsqrt(jnp.mean(centred * centred, -1, keepdims=True) + EPS)
    return centred * scale, scale


def norm_back(grad, hat, scale, gain):
    hat_grad = grad * gain
    return scale * (
        hat_grad
        - jnp.mean(hat_grad, -1, keepdims=True)
        - hat * jnp.mean(hat_grad * hat, -1, keepdims=True)
    )


def label_column(seg):
    rows = seg.shape[1]
    return jnp.transpose(jnp.broadcast_to(seg[...].astype(F32), (128, rows)))


def block_projection(proj):
    tall = jnp.concatenate([proj[...]] * 4, axis=0)
    wide = jnp.concatenate([tall] * 4, axis=1)
    group = lax.broadcasted_iota(jnp.int32, (256, 128), 0) // HD
    feat = lax.broadcasted_iota(jnp.int32, (256, 128), 1) // FEAT
    return jnp.where(group == feat, wide, 0.0), jnp.where(group == feat, 1.0, 0.0).astype(BF16)


def turn(u, cos, sin_a, sin_b):
    return u * cos + pltpu.roll(u, 96, 1) * sin_a + pltpu.roll(u, 32, 1) * sin_b


def turn_back(u, cos, sin_a, sin_b):
    return u * cos - pltpu.roll(u, 96, 1) * sin_a - pltpu.roll(u, 32, 1) * sin_b


class Feed:
    def __init__(self, pairs, sems):
        self.copies = [pltpu.make_async_copy(src, dst, sems.at[n]) for n, (src, dst) in enumerate(pairs)]
        for copy in self.copies:
            copy.start()
        self.left = list(range(len(self.copies)))

    def need(self, *which):
        for n in which:
            if n in self.left:
                self.copies[n].wait()
                self.left.remove(n)


class Drain:
    def __init__(self, sems):
        self.sems, self.copies = sems, []

    def put(self, src, dst):
        copy = pltpu.make_async_copy(src, dst, self.sems.at[len(self.copies)])
        copy.start()
        self.copies.append(copy)

    def end(self):
        for copy in self.copies:
            copy.wait()


def call(kernel, name, ins, outs, scratch, n_in, n_out, limit, smem=0, cost=0, trans=0, moved=0):
    return pl.pallas_call(
        kernel,
        out_shape=outs,
        in_specs=[SMEM] * smem + [ANY] * (len(ins) - smem),
        out_specs=[ANY] * len(outs),
        scratch_shapes=list(scratch) + [pltpu.SemaphoreType.DMA((n_in,)), pltpu.SemaphoreType.DMA((n_out,))],
        compiler_params=pltpu.CompilerParams(vmem_limit_bytes=limit << 20),
        cost_estimate=pl.CostEstimate(flops=cost, bytes_accessed=moved, transcendentals=trans),
        name=name,
    )(*ins)


FWD_IN = 16
FWD_OUT = 10


def attn_fwd_kernel(*refs):
    ins, outs = refs[:FWD_IN], refs[FWD_IN:FWD_IN + FWD_OUT]
    held = refs[FWD_IN + FWD_OUT:FWD_IN + FWD_OUT + FWD_IN]
    res = refs[2 * FWD_IN + FWD_OUT:2 * FWD_IN + 2 * FWD_OUT]
    col_s, in_sem, out_sem = refs[2 * FWD_IN + 2 * FWD_OUT:]
    feed = Feed(list(zip(ins, held)), in_sem)
    drain = Drain(out_sem)
    tok, seg, fg, fb, wv, wq, bq, wk, bk, tab, proj, wo, bv, bo, sg, sb = (held[n] for n in range(16))
    normed_o, s_o, f_o, v_o, c0_o, ctx_o, dinv_o, mid_o, sec_o, rot_o = res
    rows, width = tok.shape
    feed.need(1, 9)
    col_s[...] = label_column(seg)
    seg_row = seg[...].astype(F32)
    less = jnp.where(seg_row < col_s[:, :1], 1.0, 0.0)
    start = jnp.sum(less, axis=1, keepdims=True)
    place = lax.broadcasted_iota(jnp.int32, (rows, 1), 0).astype(F32) - start
    length = tab.shape[1]
    ladder = lax.broadcasted_iota(jnp.int32, (rows, length), 1).astype(F32)
    one_hot = jnp.where(ladder == place, 1.0, 0.0).astype(BF16)
    rot_o[...] = nn(one_hot, tab[0]) + nn(one_hot, tab[1]) + nn(one_hot, tab[2])

    feed.need(*range(12))
    p_wide, blocks = block_projection(proj)
    p_hi, p_lo = split(p_wide)
    halves = blocks * 0.5

    tile = 256

    def first(i, _):
        at = pl.ds(pl.multiple_of(i * tile, tile), tile)
        x = tok[at, :].astype(F32)
        hat, _scale = norm_parts(x)
        normed = (hat * fg[...] + fb[...]).astype(BF16)
        normed_o[at, :] = normed
        v_o[at, :] = nn(normed, wv[...]).astype(BF16)
        cos, sin_a, sin_b = rot_o[at, 0:128], rot_o[at, 128:256], rot_o[at, 256:384]
        for which, (w, b) in enumerate(((wq, bq), (wk, bk))):
            u = nn(normed, w[...]) + b[...]
            for j in range(width // 128):
                lanes = slice(128 * j, 128 * j + 128)
                s_o[which, at, lanes] = turn(u[:, lanes], cos, sin_a, sin_b)
            for g in range(width // 256):
                s = s_o[which, at, 256 * g:256 * g + 256]
                s_hi, s_lo = split(s)
                q_hi, q_lo = split(s * s)
                e = nn(s_hi, p_hi) + nn(s_lo, p_hi) + nn(s_hi, p_lo) - nn(q_hi, halves) - nn(q_lo, halves)
                f_o[which, at, 128 * g:128 * g + 128] = (jnp.exp(e) * FEAT ** -0.5).astype(BF16)
        return 0

    lax.fori_loop(0, rows // tile, first, 0)
    drain.put(rot_o, outs[9])
    drain.put(normed_o, outs[0])
    drain.put(s_o, outs[1])
    drain.put(f_o, outs[2])
    drain.put(v_o, outs[3])
    feed.need(*range(16))

    ones = jnp.ones((rows, 128), BF16)
    even = lax.broadcasted_iota(jnp.int32, (1, 128), 1) < HD

    def second(i, _):
        at = pl.ds(pl.multiple_of(i * tile, tile), tile)
        same = col_s[at, :1] == seg_row
        for j in range(HEADS // 2):
            g = j // 2
            vals = jnp.concatenate([v_o[:, 128 * j:128 * j + 128], ones], 1)
            qf = f_o[0, at, 128 * g:128 * g + 128]
            kf = f_o[1, :, 128 * g:128 * g + 128]
            res = []
            for h in range(2):
                scores = nt(qf * lane_mask(2 * (j % 2) + h), kf)
                weights = jnp.where(same, scores, 0.0).astype(BF16)
                res.append(nn(weights, vals))
            num = jnp.where(even, res[0][:, :128], res[1][:, :128])
            inv = 1.0 / jnp.where(even, res[0][:, 128:], res[1][:, 128:])
            lanes = slice(128 * j, 128 * j + 128)
            ctx = num * inv
            dinv_o[at, lanes] = inv
            c0_o[at, lanes] = ctx
            ctx_o[at, lanes] = (ctx + bv[:, lanes]).astype(BF16)
        middle = tok[at, :].astype(F32) + nn(ctx_o[at, :], wo[...]) + bo[...]
        mid_o[at, :] = middle
        hat, _scale = norm_parts(middle)
        sec_o[at, :] = (hat * sg[...] + sb[...]).astype(BF16)
        return 0

    lax.fori_loop(0, rows // tile, second, 0)
    for n in (8, 7, 4, 5, 6):
        drain.put(res[n], outs[n])
    drain.end()


def attn_fwd(tok, seg, tab, proj, fg, fb, wq, wk, wv, wo, bq, bk, bv, bo, sg, sb):
    rows, width = tok.shape
    sd = jax.ShapeDtypeStruct
    outs = (
        sd((rows, width), BF16),
        sd((2, rows, width), F32),
        sd((2, rows, HEADS * FEAT), BF16),
        sd((rows, width), BF16),
        sd((rows, width), F32),
        sd((rows, width), BF16),
        sd((rows, width), F32),
        sd((rows, width), F32),
        sd((rows, width), BF16),
        sd((rows, 384), F32),
    )
    ins = (tok, seg, fg, fb, wv, wq, bq, wk, bk, tab, proj, wo, bv, bo, sg, sb)
    scratch = [pltpu.VMEM(v.shape, v.dtype) for v in ins + outs] + [pltpu.VMEM((rows, 128), F32)]
    return call(attn_fwd_kernel, "attn_fwd", ins, outs, scratch, len(ins), len(outs), 40,
                cost=5_000_000_000, moved=20_000_000)


FFN_STEP = 256


def ffn_kernel(first, last, *refs):
    n_in = 8 if first else 10
    place, ins, refs = refs[0], refs[1:1 + n_in], refs[1 + n_in:]
    outs, refs = refs[:5], refs[5:]
    sec, cot, wu, wd, bu, oacc, sacc, oout, gup, gdn, gb, secT, in_sem, out_sem = refs
    x, y, c = place[0], place[1], place[2]
    rows, width = sec.shape
    quarter = width // 4

    def part(a, core):
        return pl.ds(pl.multiple_of((2 * a + core) * quarter, quarter), quarter)

    if first:
        sec_i, cot_i, wu_i, wd_i, bu_i, oacc_i, bd_i = ins[:7]
        pairs = [(wu_i, wu), (sec_i, sec), (bu_i, bu.at[0:1]), (cot_i, cot), (wd_i, wd), (oacc_i, oacc), (bd_i, bu.at[8:9])]
        early, more = (0, 1, 2), (3, 4)
    else:
        sec_i, cot_i, own, own_x, own_y, far, far_x, far_y, oacc_i, sacc_i = ins
        up, down = pl.ds(0, quarter), pl.ds(quarter, quarter)
        pairs = [
            (own.at[up], wu.at[part(x, c)]), (own_x, wu.at[part(1 - x, c)]),
            (far.at[up], wu.at[part(x, 1 - c)]), (far_x, wu.at[part(1 - x, 1 - c)]),
            (sec_i, sec), (own.at[pl.ds(2 * quarter, 16)], bu),
            (cot_i, cot),
            (own.at[down], wd.at[part(y, c)]), (own_y, wd.at[part(1 - y, c)]),
            (far.at[down], wd.at[part(y, 1 - c)]), (far_y, wd.at[part(1 - y, 1 - c)]),
            (oacc_i, oacc), (sacc_i, sacc),
        ]
        early, more = tuple(range(6)), tuple(range(6, 11))
    feed = Feed(pairs, in_sem)
    drain = Drain(out_sem)
    feed.need(*early)
    if first:
        bias = bu[0:1, :]
    else:
        bias = bu[0:1, :].astype(F32) + bu[1:2, :].astype(F32) + bu[2:3, :].astype(F32)
    secT[...] = jnp.transpose(sec[...])
    for n, at in enumerate(range(0, width, FFN_STEP)):
        cs = slice(at, at + FFN_STEP)
        inner = nn(sec[...], wu[:, cs]) + bias[:, cs]
        cdf = 0.5 + 0.5 * lax.erf(inner * math.sqrt(0.5))
        slope = cdf + inner * (jnp.exp(-0.5 * inner * inner) * (1.0 / math.sqrt(2.0 * math.pi)))
        hidden = (inner * cdf).astype(BF16)
        feed.need(*more)
        grad = (nt(cot[...], wd[cs, :]) * slope).astype(BF16)
        gb[:, cs] = jnp.sum(grad.astype(F32), 0, keepdims=True)
        more_out = nn(hidden, wd[cs, :])
        more_sg = nt(grad, wu[:, cs])
        feed.need(*range(len(pairs)))
        if n == 0 and first:
            oacc[...] = oacc[...] + bu[8:9, :] + more_out
            sacc[...] = more_sg
        else:
            oacc[...] += more_out
            sacc[...] += more_sg
        gdn[cs, :] = nn(jnp.transpose(hidden), cot[...]).astype(BF16)
        gup[:, cs] = nn(secT[...], grad).astype(BF16)
    half = width // 2
    mine = pl.ds(pl.multiple_of(c * half, half), half)
    other = pl.ds(pl.multiple_of((1 - c) * half, half), half)
    drain.put(gup.at[other], outs[2].at[0])
    drain.put(gdn.at[other], outs[2].at[1])
    drain.put(gup.at[mine], outs[3].at[0])
    drain.put(gdn.at[mine], outs[3].at[1])
    drain.put(sacc, outs[1])
    if last:
        oout[...] = oacc[...].astype(BF16)
        drain.put(oout, outs[0])
    else:
        drain.put(oacc, outs[0])
    drain.put(gb, outs[4])
    drain.end()


def ffn(first, last, place, *ins):
    rows, width = ins[0].shape
    sd = jax.ShapeDtypeStruct
    v = pltpu.VMEM
    outs = (
        sd((rows, width), BF16 if last else F32),
        sd((rows, width), F32),
        sd((2, width // 2, width), BF16),
        sd((2, width // 2, width), BF16),
        sd((1, width), F32),
    )
    scratch = [
        v((rows, width), BF16), v((rows, width), BF16), v((width, width), BF16), v((width, width), BF16),
        v((16, width), F32 if first else BF16), v((rows, width), F32), v((rows, width), F32), v((rows, width), BF16),
        v((width, width), BF16), v((width, width), BF16), v((1, width), F32), v((width, rows), BF16),
    ]
    return call(partial(ffn_kernel, first, last), "ffn", (place,) + ins, outs, scratch, 13, 7, 32, smem=1,
                cost=3_600_000_000, moved=12_000_000)


BWD_IN = 20


def attn_bwd_kernel(place, *refs):
    ins, outs = refs[:BWD_IN], refs[BWD_IN:BWD_IN + 4]
    held, refs = refs[BWD_IN + 4:2 * BWD_IN + 4], refs[2 * BWD_IN + 4:]
    gtok_s, gw_s, vec, col_s, cg_s, qg_s, de_s, mg_s, tr_s, in_sem, out_sem = refs
    sgrad, mid, sg, cot, ctx, wo, seg, dinv, c0, vals, f, s, rot, proj, normed, tok, fg, wq, wk, wv = held
    c = place[2]
    feed = Feed(list(zip(ins, held)), in_sem)
    drain = Drain(out_sem)
    rows, width = tok.shape
    half = width // 2
    mine = pl.ds(pl.multiple_of(c * half, half), half)
    other = pl.ds(pl.multiple_of((1 - c) * half, half), half)
    feed.need(0, 1, 2, 3)
    hat, scale = norm_parts(mid[...])
    up = sgrad[...]
    vec[...] = jnp.zeros_like(vec)
    vec[0:1, :] = jnp.sum(up * hat, 0, keepdims=True)
    vec[1:2, :] = jnp.sum(up, 0, keepdims=True)
    g = cot[...].astype(F32)
    vec[2:3, :] = jnp.sum(g, 0, keepdims=True)
    mg = g + norm_back(up, hat, scale, sg[...])
    mg_s[...] = mg
    og = mg.astype(BF16)
    vec[3:4, :] = jnp.sum(og.astype(F32), 0, keepdims=True)
    feed.need(4, 5)
    tr_s[...] = jnp.transpose(ctx[...])
    gw_s[3] = nn(tr_s[...], og).astype(BF16)
    drain.put(gw_s.at[3, other], outs[1].at[3])
    drain.put(gw_s.at[3, mine], outs[2].at[3])
    cg_s[...] = nt(og, wo[...])

    feed.need(*range(11))
    col_s[...] = label_column(seg)
    seg_row = seg[...].astype(F32)
    ones = jnp.ones((rows, 128), BF16)
    lane = lax.broadcasted_iota(jnp.int32, (1, 128), 1)
    tile = 256

    def heads(i, _):
        at = pl.ds(pl.multiple_of(i * tile, tile), tile)
        same = col_s[at, :1] == seg_row
        for j in range(HEADS // 2):
            gr = j // 2
            lanes = slice(128 * j, 128 * j + 128)
            flanes = slice(128 * gr, 128 * gr + 128)
            v_all = jnp.concatenate([vals[:, lanes], ones], 1)
            v_at = jnp.concatenate([vals[at, lanes], ones[:tile]], 1)

            def scaled(span):
                low = (cg_s[span, lanes] * dinv[span, lanes]).astype(BF16)
                less = -(low.astype(F32) * c0[span, lanes])
                hi = less.astype(BF16).astype(F32)
                return low, hi, pltpu.roll(less - hi, 64, 1)

            g_all, hi_all, lo_all = scaled(slice(None))
            g_at, hi_at, lo_at = scaled(at)
            qf_all, kf_all = f[0, :, flanes], f[1, :, flanes]
            kf_at = f[1, at, flanes]
            res_v, dq, dk = [], None, None
            for h in range(2):
                fm = lane_mask(2 * (j % 2) + h)
                own = lane // HD == h
                vm = own.astype(F32).astype(BF16)
                wT = jnp.where(same, nt(kf_at * fm, qf_all), 0.0).astype(BF16)
                res_v.append(nn(wT, g_all))
                ga = jnp.concatenate([g_all * vm, jnp.where(own, hi_all, lo_all).astype(BF16)], 1)
                dwT = jnp.where(same, nt(v_at, ga), 0.0).astype(BF16)
                gk = nn(dwT, qf_all) * fm.astype(F32)
                dk = gk if dk is None else dk + gk
                gt = jnp.concatenate([g_at * vm, jnp.where(own, hi_at, lo_at).astype(BF16)], 1)
                dw = jnp.where(same, nt(gt, v_all), 0.0).astype(BF16)
                gq = nn(dw, kf_all) * fm.astype(F32)
                dq = gq if dq is None else dq + gq
            qg_s[2, at, lanes] = jnp.where(lane < HD, res_v[0], res_v[1]).astype(BF16)
            if j % 2 == 0:
                de_s[0, at, flanes] = dq
                de_s[1, at, flanes] = dk
            else:
                de_s[0, at, flanes] = (de_s[0, at, flanes] + dq) * f[0, at, flanes].astype(F32)
                de_s[1, at, flanes] = (de_s[1, at, flanes] + dk) * f[1, at, flanes].astype(F32)
        return 0

    lax.fori_loop(0, rows // tile, heads, 0)
    feed.need(*range(BWD_IN))

    tr_s[...] = jnp.transpose(normed[...])
    gw_s[2] = nn(tr_s[...], qg_s[2]).astype(BF16)
    drain.put(gw_s.at[2, other], outs[1].at[2])
    drain.put(gw_s.at[2, mine], outs[2].at[2])

    p_wide, blocks = block_projection(proj)
    p_hi, p_lo = split(p_wide)

    def back(i, _):
        at = pl.ds(pl.multiple_of(i * tile, tile), tile)
        cos, sin_a, sin_b = rot[at, 0:128], rot[at, 128:256], rot[at, 256:384]
        for which in range(2):
            for gr in range(width // 256):
                d_hi, d_lo = split(de_s[which, at, 128 * gr:128 * gr + 128])
                s_at = s[which, at, 256 * gr:256 * gr + 256]
                ds = nt(d_hi, p_hi) + nt(d_lo, p_hi) + nt(d_hi, p_lo) - s_at * (nt(d_hi, blocks) + nt(d_lo, blocks))
                for k in range(2):
                    du = turn_back(ds[:, 128 * k:128 * k + 128], cos, sin_a, sin_b)
                    lanes = slice(256 * gr + 128 * k, 256 * gr + 128 * k + 128)
                    qg_s[which, at, lanes] = du.astype(BF16)
        return 0

    lax.fori_loop(0, rows // tile, back, 0)

    for which in range(2):
        gw_s[which] = nn(tr_s[...], qg_s[which]).astype(BF16)
        drain.put(gw_s.at[which, other], outs[1].at[which])
        drain.put(gw_s.at[which, mine], outs[2].at[which])
    for which in range(3):
        vec[4 + which:5 + which, :] = jnp.sum(qg_s[which].astype(F32), 0, keepdims=True)
    hat1, scale1 = norm_parts(tok[...].astype(F32))
    ng = nt(qg_s[0], wq[...]) + nt(qg_s[1], wk[...]) + nt(qg_s[2], wv[...])
    vec[7:8, :] = jnp.sum(ng * hat1, 0, keepdims=True)
    vec[8:9, :] = jnp.sum(ng, 0, keepdims=True)
    gtok_s[...] = (mg_s[...] + norm_back(ng, hat1, scale1, fg[...])).astype(BF16)
    drain.put(gtok_s, outs[0])
    drain.put(vec, outs[3])
    drain.end()


def attn_bwd(place, sgrad, mid, sg, cot, ctx, wo, seg, dinv, c0, vals, f, s, rot, proj, normed, tok, fg, wq, wk, wv):
    rows, width = tok.shape
    sd = jax.ShapeDtypeStruct
    ins = (sgrad, mid, sg, cot, ctx, wo, seg, dinv, c0, vals, f, s, rot, proj, normed, tok, fg, wq, wk, wv)
    outs = (
        sd((rows, width), BF16),
        sd((4, width // 2, width), BF16),
        sd((4, width // 2, width), BF16),
        sd((16, width), F32),
    )
    scratch = [pltpu.VMEM(v.shape, v.dtype) for v in ins] + [
        pltpu.VMEM((rows, width), BF16),
        pltpu.VMEM((4, width, width), BF16),
        pltpu.VMEM((16, width), F32),
        pltpu.VMEM((rows, 128), F32),
        pltpu.VMEM((rows, width), F32),
        pltpu.VMEM((3, rows, width), BF16),
        pltpu.VMEM((2, rows, HEADS * FEAT), F32),
        pltpu.VMEM((rows, width), F32),
        pltpu.VMEM((width, rows), BF16),
    ]
    return call(attn_bwd_kernel, "attn_bwd", (place,) + ins, outs, scratch, BWD_IN, 10, 54, smem=1,
                cost=20_000_000_000, moved=30_000_000)


def add_low(a, b):
    return (a.astype(F32) + b.astype(F32)).astype(BF16)


class Links:
    def __init__(self):
        self.dp, self.ring = lax.axis_size("dp"), lax.axis_size("tensor")
        self.at = lax.axis_index("dp")
        self.z = lax.axis_index("tensor")
        self.bits = [1 << n for n in range(1, self.dp.bit_length() - 1)]

    def side(self, bit):
        return (self.at // bit) % 2

    def swap(self, v, bit):
        return lax.ppermute(v, "dp", [(i, i ^ bit) for i in range(self.dp)])

    def shift(self, v):
        return lax.ppermute(v, "tensor", [(i, (i + 1) % self.ring) for i in range(self.ring)])

    def halve(self, v, bit):
        send = lax.dynamic_index_in_dim(v, 1 - self.side(bit), v.ndim - 3, keepdims=False)
        keep = lax.dynamic_index_in_dim(v, self.side(bit), v.ndim - 3, keepdims=False)
        return add_low(keep, self.swap(send, bit))


def cut_rows(v):
    return v.reshape(v.shape[:-2] + (2, v.shape[-2] // 2, v.shape[-1]))


def sum_halves(links, a, b):
    for up, down in zip(links.bits, links.bits[::-1]):
        a, b = links.halve(cut_rows(a), up), links.halve(cut_rows(b), down)
    return a, b


def spread_rows(links, v, lead, upwards):
    n = links.dp.bit_length() - 1
    rows, width = v.shape[-2:]
    v = v.reshape((2,) * n + lead + (rows, width))
    axes = list(range(n))[::-1]
    order = [axes[0]] + (axes[1:] if upwards else axes[1:][::-1])
    perm = [n + i for i in range(len(lead))] + order + [n + len(lead), n + len(lead) + 1]
    return v.transpose(perm).reshape(lead + (rows << n, width))


def body(tokens, cotangent, segment, projection, first_gain, first_bias, w_query, w_key, w_value, w_out,
         b_query, b_key, b_value, b_out, second_gain, second_bias, w_up, b_up, w_down, b_down):
    links = Links()
    rows, width = tokens.shape
    low_bit, top_bit = links.bits[0], links.bits[-1]
    core, x, y = links.side(1), links.side(low_bit), links.side(top_bit)
    place = jnp.stack([x, y, core]).astype(jnp.int32)
    quarter = width // 4

    def line(v):
        return v.reshape(1, -1)

    bias_parts, left = [], b_up
    for _ in range(3):
        part = lax.reduce_precision(left, 8, 7)
        bias_parts.append(part.astype(BF16))
        left = left - part
    share = jnp.concatenate([
        lax.dynamic_slice_in_dim(w_up, (2 * x + core) * quarter, quarter, 0),
        lax.dynamic_slice_in_dim(w_down, (2 * y + core) * quarter, quarter, 0),
        jnp.stack(bias_parts + [jnp.zeros_like(bias_parts[0])] * 13),
    ])
    slices = []
    for _ in range(links.ring - 1):
        share = links.shift(share)
        far = links.swap(share, 1)
        own_x = links.swap(share[:quarter], low_bit)
        own_y = links.swap(share[quarter:2 * quarter], top_bit)
        slices.append((share, own_x, own_y, far, links.swap(own_x, 1), links.swap(own_y, 1)))

    table = jnp.asarray(rotary_table(256))
    normed, s, f, vals, c0, ctx, dinv, mid, second, rot = attn_fwd(
        tokens, segment, table, projection, line(first_gain), line(first_bias), w_query, w_key, w_value, w_out,
        line(b_query), line(b_key), line(b_value), line(b_out), line(second_gain), line(second_bias))

    sums, slopes = [], []
    out, sgrad, send, keep, slope = ffn(True, False, place, second, cotangent, w_up, w_down, line(b_up), mid, line(b_down), mid)
    sums.append(add_low(keep, links.swap(send, 1)))
    slopes.append(slope)
    for n, parts in enumerate(slices):
        out, sgrad, send, keep, slope = ffn(False, n == len(slices) - 1, place, second, cotangent, *parts, out, sgrad)
        sums.append(add_low(keep, links.swap(send, 1)))
        slopes.append(slope)

    total = sums[1]
    for n in list(range(2, links.ring)) + [0]:
        total = add_low(links.shift(total), sums[n])
    up_part, down_part = sum_halves(links, total[0], total[1])
    both = lax.all_gather(jnp.stack([up_part, down_part]), "dp", axis=0)
    grad_w_up = spread_rows(links, both[:, 0], (), True).astype(F32)
    grad_w_down = spread_rows(links, both[:, 1], (), False).astype(F32)

    grad_tokens, send, keep, vec = attn_bwd(
        place, sgrad, mid, line(second_gain), cotangent, ctx, w_out, segment, dinv, c0, vals, f, s, rot, projection,
        normed, tokens, line(first_gain), w_query, w_key, w_value)
    mats = add_low(keep, links.swap(send, 1))
    a, b = sum_halves(links, mats[:2], mats[2:])
    a = a.reshape(links.ring, -1, width)
    b = b.reshape(links.ring, -1, width)
    ab = jnp.stack([a, b], 1)

    def piece(n):
        return lax.dynamic_index_in_dim(ab, (links.z - n) % links.ring, 0, keepdims=False)

    total = piece(1)
    for n in list(range(2, links.ring)) + [0]:
        total = add_low(links.shift(total), piece(n))
    whole = lax.all_gather(total, ("dp", "tensor"), axis=0)
    whole = whole.reshape(links.dp, 2, links.ring // 2, 2, -1, width)
    whole = whole.transpose(0, 3, 1, 2, 4, 5).reshape(links.dp, 2, 2, -1, width)
    first_two = spread_rows(links, whole[:, 0], (2,), True).astype(F32)
    last_two = spread_rows(links, whole[:, 1], (2,), False).astype(F32)

    slope_all = jnp.zeros((links.ring, width), F32)
    for n, slope in enumerate(slopes):
        slope_all = lax.dynamic_update_slice_in_dim(slope_all, slope, (links.z - n) % links.ring, 0)
    vec = lax.psum(jnp.concatenate([vec, slope_all]), ("dp", "tensor"))
    grad_b_up = lax.dynamic_index_in_dim(vec, 16 + links.z, 0, keepdims=False)
    return (
        out, grad_tokens, vec[7], vec[8], first_two[0], first_two[1], last_two[0], last_two[1],
        vec[4], vec[5], vec[6], vec[3], vec[0], vec[1], grad_w_up, grad_b_up, grad_w_down, vec[2],
    )


def solution(mesh):
    rows = P(("dp", "tensor"), None)
    whole = P()
    return jax.shard_map(
        body,
        mesh=mesh,
        in_specs=(rows,) * 3 + (whole,) * 13 + (P(None, "tensor"), P("tensor"), P("tensor", None), whole),
        out_specs=(rows,) * 2 + (whole,) * 12 + (P(None, "tensor"), P("tensor"), P("tensor", None), whole),
        check_vma=False,
    )
```

time: 661 us -> 350 us (0.53)
  waiting for transfers between devices: 378 us -> 155 us
  matrix products: 144 us -> 0 us
  Pallas kernels: 0 us -> 75.5 us
  starting transfers between devices: 0.65 us -> 21.3 us
  blocking collectives: 57 us -> 39.7 us
  other arithmetic: 22.8 us -> 11 us
  local copies, waits for them, and re-layouts: 34.7 us -> 26.6 us
    psum x2 -> x0, waiting for transfers between devices: 159 us -> none  [the longest x1 159 us: body(): lax.psum((gain_one_grad, bias_one_grad, query_weight_grad, wkey_grad, val...]
    dot_general x28 -> x0, matrix products: 144 us -> none  [the longest x3 34.1 us: attend(): jnp.einsum('otg,atg->toa', query_feature_map, key_feature_map, precision=...]
    ppermute x0 -> x37, waiting for transfers between devices: none -> 138 us  [the longest x9 79.5 us: shift(): lax.ppermute(v, 'tensor', [(i, (i + 1) % self.ring) for i in range(self.r...]
    all_gather x2, waiting for transfers between devices: 122 us -> 16.5 us  [the longest x1 16.5 us: body(): whole = lax.all_gather(total, ('dp', 'tensor'), axis=0)]
    reduce_scatter x2 -> x0, waiting for transfers between devices: 96.1 us -> none  [the longest x1 60.1 us: body(): lax.psum_scatter(matmul(lax.slice_in_dim(hidden_low, 0, row_count * lax.a...]
    pallas_call x0 -> x6, Pallas kernels: none -> 75.5 us  [call(): pl.pallas_call(kernel, out_shape=outs, in_specs=[SMEM] * smem + [ANY] * (...]
    ppermute x0 -> x37, starting transfers between devices: none -> 21.2 us  [the longest x28 16.6 us: swap(): return lax.ppermute(v, 'dp', [(i, i ^ bit) for i in range(self.dp)])]
    psum x2 -> x1, blocking collectives: 57 us -> 39.7 us  [body(): vec = lax.psum(jnp.concatenate([vec, slope_all]), ('dp', 'tensor'))]
  transfers between devices with their start and end apart: 6 -> 39, of which waited for: 5 -> 24; matrix products, arithmetic and copies ran while one was open for 16% -> 5% of each run, Pallas kernels for 0% -> 22%
where the time goes in v1:
time: 350 us; the launch traced here: 344 us
  waiting for transfers between devices  155 us (44%)
  Pallas kernels  75.5 us (22%)
  blocking collectives  39.7 us (11%)
  local copies, waits for them, and re-layouts  26.6 us (8%)
  starting transfers between devices  21.3 us (6%)
  between operations  15.7 us (4%)
  other arithmetic  11 us (3%)
    ppermute x9, waiting for transfers between devices, shift(): lax.ppermute(v, 'tensor', [(i, (i + 1) % self.ring) for i in range(self.r...  79.5 us
    pallas_call x6, Pallas kernels, call(): pl.pallas_call(kernel, out_shape=outs, in_specs=[SMEM] * smem + [ANY] * (...  75.5 us
    ppermute x28, waiting for transfers between devices, swap(): return lax.ppermute(v, 'dp', [(i, i ^ bit) for i in range(self.dp)])  58.5 us
    psum x1, blocking collectives, body(): vec = lax.psum(jnp.concatenate([vec, slope_all]), ('dp', 'tensor'))  39.7 us
    ppermute x28, starting transfers between devices, swap(): return lax.ppermute(v, 'dp', [(i, i ^ bit) for i in range(self.dp)])  16.6 us
    all_gather x1, waiting for transfers between devices, body(): whole = lax.all_gather(total, ('dp', 'tensor'), axis=0)  16.5 us
    unnamed x73, local copies, waits for them, and re-layouts  8.13 us
    convert_element_type x14, other arithmetic, add_low(): return (a.astype(F32) + b.astype(F32)).astype(BF16)  7.95 us
  transfers between devices with their start and end apart: 39, of which 24 were waited for; matrix products, arithmetic and copies ran while one was open for 5% of the time, Pallas kernels for 22%

profile of v1, /device:TPU:0, one launch (start us, length us, event | category | flops | bytes accessed | tf_op | source)
XLA Modules:
  0.0 344.3 jit_solution(12384339193879792054)
XLA Ops:
  9.7 3.1 collective-permute-start
  13.1 15.6 %collective-permute-done.refs_3_ = bf16[400,768]{1,0:T(8,128)(2,1)S(1)} collective-permute-done((bf16[400,768]{1,0:T(8,128)(2,1)S(1)}, bf16[400,768]{1,0:T(8,128)(2,1)S(1)}, u32[]{:S(2)}, u32[]{:S(2)}) %collective-permute-start) | collective-permute-done | bytes 614432 | tf_op jit(solution)/shard_map/ppermute | solution.py:521
  36.7 14.7 %attn_fwd.1 = (bf16[512,768]{1,0:T(8,128)(2,1)S(1)}, f32[2,512,768]{2,1,0:T(8,128)}, bf16[2,512,384]{2,1,0:T(8,128)(2,1)S(1)}, bf16[512,768]{1,0:T(8,128)(2,1)S(...) custom-call(bf16[512,768]{1,0:T(8,128)(2,1)S(1)} %copy-done.10, ...), custom_call_target="tpu_custom_call" | custom-call | flops 5000000000 | bytes 20000000 | tf_op jit(solution)/shard_map/attn_fwd/pallas_call | solution.py:124
  55.9 7.5 %ffn.4 = (f32[512,768]{1,0:T(8,128)S(1)}, f32[512,768]{1,0:T(8,128)S(1)}, bf16[2,384,768]{2,1,0:T(8,128)(2,1)}, bf16[2,384,768]{2,1,0:T(8,128)(2,1)S(1)}, f32[1,768]{1,0:T(1,128)S(1)}) custom-call(s32[3]{0:T(128)S(1)} %pad_add_fusion.refs_0_.place, bf16[512,768]{1,0:T(8,128)(2,1)S(1)} %get-tuple-element.52.refs_1_, bf16[512,768]{1,0:T(8,128)(2,1)S(1)} %copy-done.11, ...), custom_call_target="tpu_custom_call" | custom-call | flops 3600000000 | bytes 12000000 | tf_op jit(solution)/shard_map/ffn/pallas_call | solution.py:124
  63.5 7.4 %ffn.5 = (f32[512,768]{1,0:T(8,128)S(1)}, f32[512,768]{1,0:T(8,128)S(1)}, bf16[2,384,768]{2,1,0:T(8,128)(2,1)S(1)}, bf16[2,384,768]{2,1,0:T(8,128)(2,1)S(1)}, f32[1,768]{1,0:T(1,128)S(1)}) custom-call(s32[3]{0:T(128)S(1)} %pad_add_fusion.refs_0_.place, bf16[512,768]{1,0:T(8,128)(2,1)S(1)} %get-tuple-element.52.refs_1_, bf16[512,768]{1,0:T(8,128)(2,1)S(1)} %copy-done.11, ...), custom_call_target="tpu_custom_call" | custom-call | flops 3600000000 | bytes 12000000 | tf_op jit(solution)/shard_map/ffn/pallas_call | solution.py:124
  72.8 8.2 %collective-permute-done.8.refs_4_ = bf16[192,768]{1,0:T(8,128)(2,1)S(1)} collective-permute-done((bf16[192,768]{1,0:T(8,128)(2,1)S(1)}, bf16[192,768]{1,0:T(8,128)(2,1)S(1)}, u32[]{:S(2)}, u32[]{:S(2)}) %collective-permute-start.8) | collective-permute-done | bytes 294944 | tf_op jit(solution)/shard_map/ppermute | solution.py:518
  83.1 7.4 %ffn.6 = (f32[512,768]{1,0:T(8,128)S(1)}, f32[512,768]{1,0:T(8,128)S(1)}, bf16[2,384,768]{2,1,0:T(8,128)(2,1)S(1)}, bf16[2,384,768]{2,1,0:T(8,128)(2,1)S(1)}, f32[1,768]{1,0:T(1,128)S(1)}) custom-call(s32[3]{0:T(128)S(1)} %pad_add_fusion.refs_0_.place, bf16[512,768]{1,0:T(8,128)(2,1)S(1)} %get-tuple-element.52.refs_1_, bf16[512,768]{1,0:T(8,128)(2,1)S(1)} %copy-done.11, ...), custom_call_target="tpu_custom_call" | custom-call | flops 3600000000 | bytes 12000000 | tf_op jit(solution)/shard_map/ffn/pallas_call | solution.py:124
  91.2 9.0 %collective-permute-done.2.refs_3_ = bf16[400,768]{1,0:T(8,128)(2,1)S(1)} collective-permute-done((bf16[400,768]{1,0:T(8,128)(2,1)S(1)}, bf16[400,768]{1,0:T(8,128)(2,1)S(1)}, u32[]{:S(2)}, u32[]{:S(2)}) %collective-permute-start.2) | collective-permute-done | bytes 614432 | tf_op jit(solution)/shard_map/ppermute | solution.py:521
  102.0 7.7 %collective-permute-done.3.refs_4_ = bf16[192,768]{1,0:T(8,128)(2,1)S(1)} collective-permute-done((bf16[192,768]{1,0:T(8,128)(2,1)S(1)}, bf16[192,768]{1,0:T(8,128)(2,1)S(1)}, u32[]{:S(2)}, u32[]{:S(2)}) %collective-permute-start.3) | collective-permute-done | bytes 294944 | tf_op jit(solution)/shard_map/ppermute | solution.py:518
  112.2 8.0 %ffn.7 = (bf16[512,768]{1,0:T(8,128)(2,1)}, f32[512,768]{1,0:T(8,128)S(1)}, bf16[2,384,768]{2,1,0:T(8,128)(2,1)}, bf16[2,384,768]{2,1,0:T(8,128)(2,1)S(1)}, f32[1,768]{1,0:T(1,128)S(1)}) custom-call(s32[3]{0:T(128)S(1)} %pad_add_fusion.refs_0_.place, bf16[512,768]{1,0:T(8,128)(2,1)S(1)} %get-tuple-element.52.refs_1_, bf16[512,768]{1,0:T(8,128)(2,1)S(1)} %copy-done.11, ...), custom_call_target="tpu_custom_call" | custom-call | flops 3600000000 | bytes 12000000 | tf_op jit(solution)/shard_map/ffn/pallas_call | solution.py:124
  120.4 4.4 %collective-permute-done.27 = bf16[2,384,768]{2,1,0:T(8,128)(2,1)S(1)} collective-permute-done((bf16[2,384,768]{2,1,0:T(8,128)(2,1)S(1)}, bf16[2,384,768]{2,1,0:T(8,128)(2,1)S(1)}, u32[]{:S(2)}, u32[]{:S(2)}) %collective-permute-start.27) | collective-permute-done | bytes 1179680 | tf_op jit(solution)/shard_map/ppermute | solution.py:521
  126.3 29.4 %collective-permute-done.29 = bf16[2,384,768]{2,1,0:T(8,128)(2,1)} collective-permute-done((bf16[2,384,768]{2,1,0:T(8,128)(2,1)}, bf16[2,384,768]{2,1,0:T(8,128)(2,1)}, u32[]{:S(2)}, u32[]{:S(2)}) %collective-permute-start.29) | collective-permute-done | bytes 1179680 | tf_op jit(solution)/shard_map/ppermute | solution.py:521
  158.1 30.5 %attn_bwd.1 = (bf16[512,768]{1,0:T(8,128)(2,1)}, bf16[4,384,768]{2,1,0:T(8,128)(2,1)}, bf16[4,384,768]{2,1,0:T(8,128)(2,1)}, f32[16,768]{1,0:T(8,128)}) custom-call(s32[3]{0:T(128)} %copy-done.5, f32[512,768]{1,0:T(8,128)} %copy-done.14, f32[512,768]{1,0:T(8,128)} %get-tuple-element.53.refs_6_.refs_8_.refs_1_, f32[1,768]{1,0:T(1,128)} %copy-done.4, ...), custom_call_target="tpu_custom_call" | custom-call | flops 20000000000 | bytes 30000000 | tf_op jit(solution)/shard_map/attn_bwd/pallas_call | solution.py:124
  191.7 7.0 %collective-permute-done.33 = bf16[192,768]{1,0:T(8,128)(2,1)S(1)} collective-permute-done((bf16[192,768]{1,0:T(8,128)(2,1)S(1)}, bf16[192,768]{1,0:T(8,128)(2,1)S(1)}, u32[]{:S(2)}, u32[]{:S(2)}) %collective-permute-start.33) | collective-permute-done | bytes 294944 | tf_op jit(solution)/shard_map/ppermute | solution.py:518
  201.4 3.1 collective-permute-done.34
  211.6 14.4 %collective-permute-done.21 = bf16[2,192,768]{2,1,0:T(8,128)(2,1)S(1)} collective-permute-done((bf16[2,192,768]{2,1,0:T(8,128)(2,1)S(1)}, bf16[2,192,768]{2,1,0:T(8,128)(2,1)S(1)}, u32[]{:S(2)}, u32[]{:S(2)}) %collective-permute-start.21) | collective-permute-done | bytes 589856 | tf_op jit(solution)/shard_map/ppermute | solution.py:518
  228.9 7.7 %collective-permute-done.22 = bf16[2,96,768]{2,1,0:T(8,128)(2,1)S(1)} collective-permute-done((bf16[2,96,768]{2,1,0:T(8,128)(2,1)S(1)}, bf16[2,96,768]{2,1,0:T(8,128)(2,1)S(1)}, u32[]{:S(2)}, u32[]{:S(2)}) %collective-permute-start.22) | collective-permute-done | bytes 294944 | tf_op jit(solution)/shard_map/ppermute | solution.py:518
  236.7 3.7 %collective-permute-done.20 = bf16[2,96,768]{2,1,0:T(8,128)(2,1)S(1)} collective-permute-done((bf16[2,96,768]{2,1,0:T(8,128)(2,1)S(1)}, bf16[2,96,768]{2,1,0:T(8,128)(2,1)S(1)}, u32[]{:S(2)}, u32[]{:S(2)}) %collective-permute-start.20) | collective-permute-done | bytes 294944 | tf_op jit(solution)/shard_map/ppermute | solution.py:518
  240.7 7.4 %collective-permute-done.23 = bf16[2,48,768]{2,1,0:T(8,128)(2,1)S(1)} collective-permute-done((bf16[2,48,768]{2,1,0:T(8,128)(2,1)S(1)}, bf16[2,48,768]{2,1,0:T(8,128)(2,1)S(1)}, u32[]{:S(2)}, u32[]{:S(2)}) %collective-permute-start.23) | collective-permute-done | bytes 147488 | tf_op jit(solution)/shard_map/ppermute | solution.py:521
  248.2 6.9 %collective-permute-done.24 = bf16[2,48,768]{2,1,0:T(8,128)(2,1)S(1)} collective-permute-done((bf16[2,48,768]{2,1,0:T(8,128)(2,1)S(1)}, bf16[2,48,768]{2,1,0:T(8,128)(2,1)S(1)}, u32[]{:S(2)}, u32[]{:S(2)}) %collective-permute-start.24) | collective-permute-done | bytes 147488 | tf_op jit(solution)/shard_map/ppermute | solution.py:521
  255.2 6.9 %collective-permute-done.25 = bf16[2,48,768]{2,1,0:T(8,128)(2,1)S(1)} collective-permute-done((bf16[2,48,768]{2,1,0:T(8,128)(2,1)S(1)}, bf16[2,48,768]{2,1,0:T(8,128)(2,1)S(1)}, u32[]{:S(2)}, u32[]{:S(2)}) %collective-permute-start.25) | collective-permute-done | bytes 147488 | tf_op jit(solution)/shard_map/ppermute | solution.py:521
  263.2 39.7 %psum.7 = f32[20,768]{1,0:T(8,128)S(1)} all-reduce(f32[20,768]{1,0:T(8,128)S(1)} %pad_maximum_fusion.1), channel_id=1, replica_groups=mesh['dp'=8,'tensor'=4] {'dp','tensor'}, use_global_device_ids=true, to_apply=%region_0.1 | all-reduce | flops 15360 | bytes 122880 | tf_op jit(solution)/shard_map/psum | solution.py:625
  308.9 16.5 %all-gather.5.cloned.1.call-done = bf16[64,48,768]{2,1,0:T(8,128)(2,1)} async-done(((bf16[2,48,768]{2,1,0:T(8,128)(2,1)}), bf16[64,48,768]{2,1,0:T(8,128)(2,1)}) %all-gather.5.cloned.1.call-update) | async-done | bytes 4718608 | tf_op jit(solution)/shard_map/all_gather | solution.py:616
  325.4 2.9 copy.62
  (209 shorter events, 59.5 us)
Async XLA Ops:
  7.3 296.3 %all-gather.7.cloned.1.call-start = ((), (), s32[]{:S(2)}) async-start(), calls=%async_computation.1 | async-start | bytes 2654208 | tf_op jit(solution)/shard_map/all_gather | solution.py:597
  9.7 19.0 %collective-permute-start = (bf16[400,768]{1,0:T(8,128)(2,1)S(1)}, bf16[400,768]{1,0:T(8,128)(2,1)S(1)}, u32[]{:S(2)}, u32[]{:S(2)}) collective-permute-start(bf16[400,768]{1,0:T(8,128)(2,1)S(1)} %concatenate.14), channel_id=1, source_target_pairs={{0,1},{1,2},{2,3},{3,0},{4,5},{5,6},{6,7},{7,4},{8,9},{9,10},{10,1... | collective-permute-start | bytes 1843208 | tf_op jit(solution)/shard_map/ppermute | solution.py:521
  28.7 24.4 %collective-permute-start.13 = (bf16[192,768]{1,0:T(8,128)(2,1)S(1)}, bf16[192,768]{1,0:T(8,128)(2,1)S(1)}, u32[]{:S(2)}, u32[]{:S(2)}) collective-permute-start(bf16[192,768]{1,0:T(8,128)(2,1)S(1)} %get-tuple-element.109), channel_id=1, source_target_pairs={{0,8},{4,12},{8,0},{12,4},{16,24},{20,28},{24,16},{28,20},{1,9},{5... | collective-permute-start | bytes 884744 | tf_op jit(solution)/shard_map/ppermute | solution.py:518
  30.3 23.4 %collective-permute-start.14 = (bf16[192,768]{1,0:T(8,128)(2,1)S(1)}, bf16[192,768]{1,0:T(8,128)(2,1)S(1)}, u32[]{:S(2)}, u32[]{:S(2)}) collective-permute-start(bf16[192,768]{1,0:T(8,128)(2,1)S(1)} %get-tuple-element.108), channel_id=1, source_target_pairs={{0,16},{4,20},{8,24},{12,28},{16,0},{20,4},{24,8},{28,12},{1,17},{... | collective-permute-start | bytes 884744 | tf_op jit(solution)/shard_map/ppermute | solution.py:518
  31.8 31.7 %collective-permute-start.15 = (bf16[400,768]{1,0:T(8,128)(2,1)S(1)}, bf16[400,768]{1,0:T(8,128)(2,1)S(1)}, u32[]{:S(2)}, u32[]{:S(2)}) collective-permute-start(bf16[400,768]{1,0:T(8,128)(2,1)S(1)} %collective-permute-done.refs_3_), channel_id=1, source_target_pairs={{0,4},{4,0},{8,12},{12,8},{16,20},{20,16},{24,28},{28,24},{1,5},{5... | collective-permute-start | bytes 1843208 | tf_op jit(solution)/shard_map/ppermute | solution.py:518
  52.5 19.0 %collective-permute-start.1 = (bf16[400,768]{1,0:T(8,128)(2,1)S(1)}, bf16[400,768]{1,0:T(8,128)(2,1)S(1)}, u32[]{:S(2)}, u32[]{:S(2)}) collective-permute-start(bf16[400,768]{1,0:T(8,128)(2,1)S(1)} %collective-permute-done.refs_3_), channel_id=1, source_target_pairs={{0,1},{1,2},{2,3},{3,0},{4,5},{5,6},{6,7},{7,4},{8,9},{9,10},{10,1... | collective-permute-start | bytes 1843208 | tf_op jit(solution)/shard_map/ppermute | solution.py:521
  53.1 10.4 %collective-permute-start.16 = (bf16[192,768]{1,0:T(8,128)(2,1)S(1)}, bf16[192,768]{1,0:T(8,128)(2,1)S(1)}, u32[]{:S(2)}, u32[]{:S(2)}) collective-permute-start(bf16[192,768]{1,0:T(8,128)(2,1)S(1)} %collective-permute-done.13.refs_4_), channel_id=1, source_target_pairs={{0,4},{4,0},{8,12},{12,8},{16,20},{20,16},{24,28},{28,24},{1,5},{5... | collective-permute-start | bytes 884744 | tf_op jit(solution)/shard_map/ppermute | solution.py:518
  53.6 9.9 %collective-permute-start.17 = (bf16[192,768]{1,0:T(8,128)(2,1)S(1)}, bf16[192,768]{1,0:T(8,128)(2,1)S(1)}, u32[]{:S(2)}, u32[]{:S(2)}) collective-permute-start(bf16[192,768]{1,0:T(8,128)(2,1)S(1)} %collective-permute-done.14.refs_5_), channel_id=1, source_target_pairs={{0,4},{4,0},{8,12},{12,8},{16,20},{20,16},{24,28},{28,24},{1,5},{5... | collective-permute-start | bytes 884744 | tf_op jit(solution)/shard_map/ppermute | solution.py:518
  70.9 19.7 %collective-permute-start.26 = (bf16[2,384,768]{2,1,0:T(8,128)(2,1)S(1)}, bf16[2,384,768]{2,1,0:T(8,128)(2,1)S(1)}, u32[]{:S(2)}, u32[]{:S(2)}) collective-permute-start(bf16[2,384,768]{2,1,0:T(8,128)(2,1)S(1)} %get-tuple-element.79), channel_id=1, source_target_pairs={{0,4},{4,0},{8,12},{12,8},{16,20},{20,16},{24,28},{28,24},{1,5},{5... | collective-permute-start | bytes 3538952 | tf_op jit(solution)/shard_map/ppermute | solution.py:518
  71.5 11.6 %collective-permute-start.10 = (bf16[400,768]{1,0:T(8,128)(2,1)S(1)}, bf16[400,768]{1,0:T(8,128)(2,1)S(1)}, u32[]{:S(2)}, u32[]{:S(2)}) collective-permute-start(bf16[400,768]{1,0:T(8,128)(2,1)S(1)} %collective-permute-done.1.refs_3_), channel_id=1, source_target_pairs={{0,4},{4,0},{8,12},{12,8},{16,20},{20,16},{24,28},{28,24},{1,5},{5... | collective-permute-start | bytes 1843208 | tf_op jit(solution)/shard_map/ppermute | solution.py:518
  81.6 18.6 %collective-permute-start.2 = (bf16[400,768]{1,0:T(8,128)(2,1)S(1)}, bf16[400,768]{1,0:T(8,128)(2,1)S(1)}, u32[]{:S(2)}, u32[]{:S(2)}) collective-permute-start(bf16[400,768]{1,0:T(8,128)(2,1)S(1)} %collective-permute-done.1.refs_3_), channel_id=1, source_target_pairs={{0,1},{1,2},{2,3},{3,0},{4,5},{5,6},{6,7},{7,4},{8,9},{9,10},{10,1... | collective-permute-start | bytes 1843208 | tf_op jit(solution)/shard_map/ppermute | solution.py:521
  90.5 30.0 %collective-permute-start.28 = (bf16[2,384,768]{2,1,0:T(8,128)(2,1)S(1)}, bf16[2,384,768]{2,1,0:T(8,128)(2,1)S(1)}, u32[]{:S(2)}, u32[]{:S(2)}) collective-permute-start(bf16[2,384,768]{2,1,0:T(8,128)(2,1)S(1)} %get-tuple-element.81), channel_id=1, source_target_pairs={{0,4},{4,0},{8,12},{12,8},{16,20},{20,16},{24,28},{28,24},{1,5},{5... | collective-permute-start | bytes 3538952 | tf_op jit(solution)/shard_map/ppermute | solution.py:518
  91.0 33.8 %collective-permute-start.27 = (bf16[2,384,768]{2,1,0:T(8,128)(2,1)S(1)}, bf16[2,384,768]{2,1,0:T(8,128)(2,1)S(1)}, u32[]{:S(2)}, u32[]{:S(2)}) collective-permute-start(bf16[2,384,768]{2,1,0:T(8,128)(2,1)S(1)} %add_convert_fusion.7), channel_id=1, source_target_pairs={{0,1},{1,2},{2,3},{3,0},{4,5},{5,6},{6,7},{7,4},{8,9},{9,10},{10,1... | collective-permute-start | bytes 3538952 | tf_op jit(solution)/shard_map/ppermute | solution.py:521
  100.2 12.0 %collective-permute-start.5 = (bf16[400,768]{1,0:T(8,128)(2,1)S(1)}, bf16[400,768]{1,0:T(8,128)(2,1)S(1)}, u32[]{:S(2)}, u32[]{:S(2)}) collective-permute-start(bf16[400,768]{1,0:T(8,128)(2,1)S(1)} %collective-permute-done.2.refs_3_), channel_id=1, source_target_pairs={{0,4},{4,0},{8,12},{12,8},{16,20},{20,16},{24,28},{28,24},{1,5},{5... | collective-permute-start | bytes 1843208 | tf_op jit(solution)/shard_map/ppermute | solution.py:518
  126.3 29.4 %collective-permute-start.29 = (bf16[2,384,768]{2,1,0:T(8,128)(2,1)}, bf16[2,384,768]{2,1,0:T(8,128)(2,1)}, u32[]{:S(2)}, u32[]{:S(2)}) collective-permute-start(bf16[2,384,768]{2,1,0:T(8,128)(2,1)} %add_convert_fusion.5), channel_id=1, source_target_pairs={{0,1},{1,2},{2,3},{3,0},{4,5},{5,6},{6,7},{7,4},{8,9},{9,10},{10,1... | collective-permute-start | bytes 3538952 | tf_op jit(solution)/shard_map/ppermute | solution.py:521
  126.3 62.4 %collective-permute-start.32 = (bf16[2,384,768]{2,1,0:T(8,128)(2,1)}, bf16[2,384,768]{2,1,0:T(8,128)(2,1)S(1)}, u32[]{:S(2)}, u32[]{:S(2)}) collective-permute-start(bf16[2,384,768]{2,1,0:T(8,128)(2,1)} %get-tuple-element.85), channel_id=1, source_target_pairs={{0,4},{4,0},{8,12},{12,8},{16,20},{20,16},{24,28},{28,24},{1,5},{5... | collective-permute-start | bytes 3538952 | tf_op jit(solution)/shard_map/ppermute | solution.py:518
  157.8 30.9 %collective-permute-start.31 = (bf16[2,384,768]{2,1,0:T(8,128)(2,1)S(1)}, bf16[2,384,768]{2,1,0:T(8,128)(2,1)S(1)}, u32[]{:S(2)}, u32[]{:S(2)}) collective-permute-start(bf16[2,384,768]{2,1,0:T(8,128)(2,1)S(1)} %add_convert_fusion.3), channel_id=1, source_target_pairs={{0,1},{1,2},{2,3},{3,0},{4,5},{5,6},{6,7},{7,4},{8,9},{9,10},{10,1... | collective-permute-start | bytes 3538952 | tf_op jit(solution)/shard_map/ppermute | solution.py:521
  188.6 17.9 %collective-permute-start.18 = (bf16[4,384,768]{2,1,0:T(8,128)(2,1)}, bf16[4,384,768]{2,1,0:T(8,128)(2,1)}, u32[]{:S(2)}, u32[]{:S(2)}) collective-permute-start(bf16[4,384,768]{2,1,0:T(8,128)(2,1)} %get-tuple-element.77), channel_id=1, source_target_pairs={{0,4},{4,0},{8,12},{12,8},{16,20},{20,16},{24,28},{28,24},{1,5},{5... | collective-permute-start | bytes 7077896 | tf_op jit(solution)/shard_map/ppermute | solution.py:518
  189.3 9.5 %collective-permute-start.33 = (bf16[192,768]{1,0:T(8,128)(2,1)S(1)}, bf16[192,768]{1,0:T(8,128)(2,1)S(1)}, u32[]{:S(2)}, u32[]{:S(2)}) collective-permute-start(bf16[192,768]{1,0:T(8,128)(2,1)S(1)} %dynamic-slice_bitcast_fusion.3), channel_id=1, source_target_pairs={{0,8},{4,12},{8,0},{12,4},{16,24},{20,28},{24,16},{28,20},{1,9},{5... | collective-permute-start | bytes 884744 | tf_op jit(solution)/shard_map/ppermute | solution.py:518
  206.4 119.0 %all-gather.5.cloned.1.call-start = ((), (), s32[]{:S(2)}) async-start(), calls=%async_computation | async-start | bytes 4866048 | tf_op jit(solution)/shard_map/all_gather | solution.py:616
  208.9 17.0 %collective-permute-start.21 = (bf16[2,192,768]{2,1,0:T(8,128)(2,1)S(1)}, bf16[2,192,768]{2,1,0:T(8,128)(2,1)S(1)}, u32[]{:S(2)}, u32[]{:S(2)}) collective-permute-start(bf16[2,192,768]{2,1,0:T(8,128)(2,1)S(1)} %dynamic-slice_bitcast_fusion), channel_id=1, source_target_pairs={{0,16},{4,20},{8,24},{12,28},{16,0},{20,4},{24,8},{28,12},{1,17},{... | collective-permute-start | bytes 1769480 | tf_op jit(solution)/shard_map/ppermute | solution.py:518
  209.8 17.9 %collective-permute-start.19 = (bf16[2,192,768]{2,1,0:T(8,128)(2,1)S(1)}, bf16[2,192,768]{2,1,0:T(8,128)(2,1)S(1)}, u32[]{:S(2)}, u32[]{:S(2)}) collective-permute-start(bf16[2,192,768]{2,1,0:T(8,128)(2,1)S(1)} %dynamic-slice_bitcast_fusion.1), channel_id=1, source_target_pairs={{0,8},{4,12},{8,0},{12,4},{16,24},{20,28},{24,16},{28,20},{1,9},{5... | collective-permute-start | bytes 1769480 | tf_op jit(solution)/shard_map/ppermute | solution.py:518
  226.1 10.5 %collective-permute-start.22 = (bf16[2,96,768]{2,1,0:T(8,128)(2,1)S(1)}, bf16[2,96,768]{2,1,0:T(8,128)(2,1)S(1)}, u32[]{:S(2)}, u32[]{:S(2)}) collective-permute-start(bf16[2,96,768]{2,1,0:T(8,128)(2,1)S(1)} %dynamic-slice_bitcast_fusion.4), channel_id=1, source_target_pairs={{0,8},{4,12},{8,0},{12,4},{16,24},{20,28},{24,16},{28,20},{1,9},{5... | collective-permute-start | bytes 884744 | tf_op jit(solution)/shard_map/ppermute | solution.py:518
  227.9 12.5 %collective-permute-start.20 = (bf16[2,96,768]{2,1,0:T(8,128)(2,1)S(1)}, bf16[2,96,768]{2,1,0:T(8,128)(2,1)S(1)}, u32[]{:S(2)}, u32[]{:S(2)}) collective-permute-start(bf16[2,96,768]{2,1,0:T(8,128)(2,1)S(1)} %dynamic-slice_bitcast_fusion.5), channel_id=1, source_target_pairs={{0,16},{4,20},{8,24},{12,28},{16,0},{20,4},{24,8},{28,12},{1,17},{... | collective-permute-start | bytes 884744 | tf_op jit(solution)/shard_map/ppermute | solution.py:518
  (51 other events, 595.1 us)
Sparse Core Ops, SparseCore 0:
  206.6 36.0 all-gather.6
  263.0 62.4 all-gather.4
